TPU v7x, 32 devices: a whole 2x2x4 slice. The times are simulated.
32 devices in a mesh: ctx: 8 (over z, x), head: 4 (over y, core).
Axes of the slice: x: 2, y: 2, z: 4, core: 2. Of those that a mesh axis runs over, the one named last changes fastest.
Arguments:
- events: bfloat16 [6144, 1024], P('ctx', 'head'), may hold values from -3 to 3
- norm_gain: float32 [1024], replicated, may hold values from 0.5 to 1.5
- w_uvqk: bfloat16 [1024, 4, 1024], P(None, None, 'head'), may hold values from -4 to 4
- w_out: bfloat16 [1024, 1024], P('head'), may hold values from -0.1875 to 0.1875
- lengths: int32 [8], replicated, may hold values from 1 to 4608, 6144 in all
Outputs:
- mixed: bfloat16 [6144, 1024], P('ctx', 'head')
Inputs may be any that keep to these rules, and one draw needn't show every extreme that they name: The lengths sum to 6144; the longest is exactly 4608.
All inputs are finite; a program needn't handle non-finite values.
Results may differ from a plain program's by a relative error of at most 0.0062.
Values may be sent and summed in bfloat16 or wider, within the bound.
A program may use at most 128 MiB of HBM per device.

v0:
```python
import jax
import jax.numpy as jnp
from jax import lax
from jax.sharding import PartitionSpec as P

D = 1024
HDIM = 128


def passed_along(value, axis, by):
    peers = lax.axis_size(axis)
    pairs = [(i, i + by) for i in range(peers) if 0 <= i + by < peers]
    return lax.ppermute(value, axis, pairs)


def attend(totals, key_block, value_block, offset, queries, query_pos, query_seg, seq_ends):
    count = key_block.shape[0]
    key_pos = offset + jnp.arange(count, dtype=jnp.int32)
    key_seg = jnp.sum((key_pos[:, None] >= seq_ends[None, :]).astype(jnp.int32), axis=1)
    score_scale = key_block.shape[-1] ** (-0.5)
    scores = (
        jnp.einsum("qhd,khd->hqk", queries, key_block, preferred_element_type=jnp.float32)
        * score_scale
    )
    allowed = (
        (query_seg[:, None] == key_seg[None, :])
        & (key_pos[None, :] <= query_pos[:, None])
        & (key_pos[None, :] >= 0)
    )
    weights = jnp.where(allowed[None], jax.nn.silu(scores), 0.0).astype(jnp.bfloat16)
    return totals + jnp.einsum(
        "hqk,khd->qhd", weights, value_block, preferred_element_type=jnp.float32
    )


def shards(events, norm_gain, w_uvqk, w_out, lengths):
    epsilon = 1e-05
    row_count = events.shape[0]
    gathered = lax.all_gather(events, "head", axis=1, tiled=True)
    xfloat = gathered.astype(jnp.float32)
    row_mean = jnp.mean(xfloat, axis=-1, keepdims=True)
    centered = xfloat - row_mean
    row_var = jnp.mean(centered * centered, axis=-1, keepdims=True)
    normed = (centered * lax.rsqrt(row_var + epsilon) * norm_gain).astype(jnp.bfloat16)
    local_cols = w_uvqk.shape[2]
    heads_here = local_cols // HDIM
    projected = jax.nn.silu(
        jnp.dot(
            normed,
            w_uvqk.reshape(w_uvqk.shape[0], 4 * local_cols),
            preferred_element_type=jnp.float32,
        )
    ).astype(jnp.bfloat16)
    projected = projected.reshape(row_count, 4, heads_here, HDIM)
    gate_rows = projected[:, 0]
    value_rows = projected[:, 1]
    queries = projected[:, 2]
    key_rows = projected[:, 3]
    seq_ends = jnp.cumsum(lengths)
    seq_starts = seq_ends - lengths
    seq_index = jnp.arange(lengths.shape[0], dtype=jnp.int32)
    my_first = lax.axis_index("ctx") * row_count
    query_pos = my_first + jnp.arange(row_count, dtype=jnp.int32)
    query_seg = jnp.sum((query_pos[:, None] >= seq_ends[None, :]).astype(jnp.int32), axis=1)
    empty = jnp.zeros((row_count, heads_here, HDIM), jnp.float32)
    ctx_count = lax.axis_size("ctx")
    device_first = jnp.arange(ctx_count, dtype=jnp.int32) * row_count
    first_seg = jnp.sum((device_first[:, None] >= seq_ends[None, :]).astype(jnp.int32), axis=1)
    start_of = jnp.sum(
        jnp.where(first_seg[:, None] == seq_index[None, :], seq_starts[None, :], 0), axis=1
    )
    reach_steps = jnp.max(jnp.arange(ctx_count, dtype=jnp.int32) - start_of // row_count)
    attended = attend(
        empty, key_rows, value_rows, my_first, queries, query_pos, query_seg, seq_ends
    )
    stacked = jnp.stack([key_rows, value_rows])

    def walk(turn_index, state):
        running, moving, offset = state
        moving = passed_along(moving, "ctx", 1)
        offset = offset - row_count
        running = attend(
            running, moving[0], moving[1], offset, queries, query_pos, query_seg, seq_ends
        )
        return (running, moving, offset)

    attended, stacked, my_offset = lax.fori_loop(
        0, reach_steps, walk, (attended, stacked, my_first)
    )
    local_squares = jnp.sum(attended * attended, axis=(1, 2))
    squares = lax.psum(local_squares, "head")
    inverse_rms = lax.rsqrt(squares / D + epsilon)
    gated = (
        (attended * inverse_rms[:, None, None] * gate_rows.astype(jnp.float32))
        .astype(jnp.bfloat16)
        .reshape(row_count, local_cols)
    )
    partial_out = jnp.dot(gated, w_out, preferred_element_type=jnp.float32)
    shared = lax.psum_scatter(partial_out, "head", scatter_dimension=1, tiled=True)
    return (events.astype(jnp.float32) + shared).astype(jnp.bfloat16)


def solution(mesh):
    in_specs = (P("ctx", "head"), P(), P(None, None, "head"), P("head", None), P())
    out_specs = P("ctx", "head")
    return jax.shard_map(shards, mesh=mesh, in_specs=in_specs, out_specs=out_specs, check_vma=False)
```

profile of v0, /device:TPU:21, one launch (start us, length us, event | category | flops | bytes accessed | tf_op | source)
XLA Modules:
  0.0 253.7 jit_solution(14238303703071802927)
XLA Ops:
  6.5 0.7 all-gather.2.cloned.1.call-update
  7.3 2.1 copy.31
  10.0 0.7 subtract_reduce_fusion
  10.7 1.4 and_and_fusion.1
  12.2 17.2 %all-gather.2.cloned.1.call-done = bf16[768,1024]{1,0:T(8,128)(2,1)} async-done(((bf16[768,256]{1,0:T(8,128)(2,1)}), bf16[768,1024]{1,0:T(8,128)(2,1)}) %all-gather.2.cloned.1.call-update) | async-done | bytes 1572880 | tf_op jit(solution)/shard_map/all_gather | solution.py:39
  29.4 1.8 convert_reduce_fusion.1
  31.2 2.0 fusion.12
  33.2 3.4 %multiply_convert_fusion = bf16[768,1024]{1,0:T(8,128)(2,1)} fusion(bf16[1024,1024]{1,0:T(8,128)(2,1)S(1)} %bitcast.51, bf16[768,1024]{1,0:T(8,128)(2,1)S(1)} %copy-done.1, f32[1024]{0:T(1024)S(1)} %copy-done.4, f32[768]{0:T(1024)S(1)} %add_rsqrt_fusion.1, f32[768]{0:T(1024)S(1)} %broadcast_multiply_fusion), kind=kOutput, calls=%fused_computation.24 | convolution fusion | flops 1618477056 | bytes 5253120 | tf_op jit(solution)/shard_map/dot_general | solution.py:48
  36.6 2.8 %reshape.221 = bf16[768,4,2,128]{3,2,1,0:T(2,128)(2,1)S(1)} reshape(bf16[768,1024]{1,0:T(8,128)(2,1)} %multiply_convert_fusion) | data formatting | bytes 3145728 | tf_op jit(solution)/shard_map/reshape | solution.py:54
  39.4 1.1 fusion.36
  40.5 0.9 copy.46
  41.5 3.6 %fusion.25 = f32[768,2,128]{0,2,1:T(8,128)S(1)} fusion(pred[768,768]{1,0:T(8,128)(4,1)} %and_and_fusion.1, bf16[768,1,2,128]{3,2,1,0:T(2,128)(2,1)} %copy-done.2, bf16[768,1,2,128]{3,2,1,0:T(2,128)(2,1)S(1)} %get-tuple-element.278, bf16[768,1,2,128]{3,2,1,0:T(2,128)(2,1)S(1)} %get-tuple-element.277), kind=kOutput, calls=%fused_computation.32 | convolution fusion | flops 612237312 | bytes 2555904 | tf_op jit(solution)/shard_map/hqk,khd->qhd/dot_general | solution.py:31
  45.3 1.0 pad_maximum_fusion
  46.3 147.1 %while.18 = (s32[]{:T(128)}, f32[768,2,128]{2,0,1:T(8,128)S(1)}, bf16[2,768,2,128]{3,1,2,0:T(8,128)(2,1)}, s32[]{:T(128)}, s32[768]{0:T(1024)S(1)}, /*index=5*/s...) while((s32[]{:T(128)}, f32[768,2,128]{2,0,1:T(8,128)S(1)}, ...), condition=%wide.region_9.10_spmd.clone.clone, body=%wide.region_7.9_spmd.clone.clone.sunk | while | flops 614813952 | bytes 8677085 | solution.py:87
  46.9 3.1 %collective-permute-start = (bf16[2,768,2,128]{3,1,2,0:T(8,128)(2,1)}, bf16[2,768,2,128]{3,1,2,0:T(8,128)(2,1)S(1)}, u32[]{:S(2)}, u32[]{:S(2)}) collective-permute-start(bf16[2,768,2,128]{3,1,2,0:T(8,128)(2,1)} %get-tuple-element.348), channel_id=1, source_target_pairs={{0,4},{4,8},{8,12},{12,16},{16,20},{20,24},{24,28},{1,5},{5,9},{9,... | collective-permute-start | bytes 2359304 | tf_op jit(solution)/shard_map/while/body/ppermute | solution.py:13
  50.1 0.6 and_and_fusion.3
  50.8 18.1 %collective-permute-done = bf16[2,768,2,128]{3,1,2,0:T(8,128)(2,1)S(1)} collective-permute-done((bf16[2,768,2,128]{3,1,2,0:T(8,128)(2,1)}, bf16[2,768,2,128]{3,1,2,0:T(8,128)(2,1)S(1)}, u32[]{:S(2)}, u32[]{:S(2)}) %collective-permute-start) | collective-permute-done | bytes 786464 | tf_op jit(solution)/shard_map/while/body/ppermute | solution.py:13
  68.8 0.9 copy.55
  69.7 3.3 %fusion.45 = f32[768,2,128]{2,0,1:T(8,128)S(1)} fusion(f32[768,2,128]{2,0,1:T(8,128)S(1)} %get-tuple-element.347, pred[768,768]{1,0:T(8,128)(4,1)S(1)} %and_and_fusion.3, bf16[768,2,128]{2,0,1:T(8,128)(2,1)} %get-tuple-element.363, bf16[2,768,2,128]{3,1,2,0:T(8,128)(2,1)S(1)} %collective-permute-done), kind=kOutput, calls=%fused_computation.6.clone.1 | convolution fusion | flops 612433920 | bytes 3342336 | tf_op jit(solution)/shard_map/while/body/hqk,khd->qhd/dot_general | solution.py:31
  73.7 2.2 collective-permute-start
  76.0 0.6 and_and_fusion.3
  76.6 18.0 %collective-permute-done = bf16[2,768,2,128]{3,1,2,0:T(8,128)(2,1)S(1)} collective-permute-done((bf16[2,768,2,128]{3,1,2,0:T(8,128)(2,1)}, bf16[2,768,2,128]{3,1,2,0:T(8,128)(2,1)S(1)}, u32[]{:S(2)}, u32[]{:S(2)}) %collective-permute-start) | collective-permute-done | bytes 786464 | tf_op jit(solution)/shard_map/while/body/ppermute | solution.py:13
  94.6 0.9 copy.55
  95.5 3.3 %fusion.45 = f32[768,2,128]{2,0,1:T(8,128)S(1)} fusion(f32[768,2,128]{2,0,1:T(8,128)S(1)} %get-tuple-element.347, pred[768,768]{1,0:T(8,128)(4,1)S(1)} %and_and_fusion.3, bf16[768,2,128]{2,0,1:T(8,128)(2,1)} %get-tuple-element.363, bf16[2,768,2,128]{3,1,2,0:T(8,128)(2,1)S(1)} %collective-permute-done), kind=kOutput, calls=%fused_computation.6.clone.1 | convolution fusion | flops 612433920 | bytes 3342336 | tf_op jit(solution)/shard_map/while/body/hqk,khd->qhd/dot_general | solution.py:31
  99.5 1.9 collective-permute-start
  101.5 0.6 and_and_fusion.3
  102.1 17.4 %collective-permute-done = bf16[2,768,2,128]{3,1,2,0:T(8,128)(2,1)S(1)} collective-permute-done((bf16[2,768,2,128]{3,1,2,0:T(8,128)(2,1)}, bf16[2,768,2,128]{3,1,2,0:T(8,128)(2,1)S(1)}, u32[]{:S(2)}, u32[]{:S(2)}) %collective-permute-start) | collective-permute-done | bytes 786464 | tf_op jit(solution)/shard_map/while/body/ppermute | solution.py:13
  119.5 0.9 copy.55
  120.4 3.3 %fusion.45 = f32[768,2,128]{2,0,1:T(8,128)S(1)} fusion(f32[768,2,128]{2,0,1:T(8,128)S(1)} %get-tuple-element.347, pred[768,768]{1,0:T(8,128)(4,1)S(1)} %and_and_fusion.3, bf16[768,2,128]{2,0,1:T(8,128)(2,1)} %get-tuple-element.363, bf16[2,768,2,128]{3,1,2,0:T(8,128)(2,1)S(1)} %collective-permute-done), kind=kOutput, calls=%fused_computation.6.clone.1 | convolution fusion | flops 612433920 | bytes 3342336 | tf_op jit(solution)/shard_map/while/body/hqk,khd->qhd/dot_general | solution.py:31
  124.3 1.9 collective-permute-start
  126.4 0.6 and_and_fusion.3
  127.0 16.5 %collective-permute-done = bf16[2,768,2,128]{3,1,2,0:T(8,128)(2,1)S(1)} collective-permute-done((bf16[2,768,2,128]{3,1,2,0:T(8,128)(2,1)}, bf16[2,768,2,128]{3,1,2,0:T(8,128)(2,1)S(1)}, u32[]{:S(2)}, u32[]{:S(2)}) %collective-permute-start) | collective-permute-done | bytes 786464 | tf_op jit(solution)/shard_map/while/body/ppermute | solution.py:13
  143.5 0.9 copy.55
  144.3 3.3 %fusion.45 = f32[768,2,128]{2,0,1:T(8,128)S(1)} fusion(f32[768,2,128]{2,0,1:T(8,128)S(1)} %get-tuple-element.347, pred[768,768]{1,0:T(8,128)(4,1)S(1)} %and_and_fusion.3, bf16[768,2,128]{2,0,1:T(8,128)(2,1)} %get-tuple-element.363, bf16[2,768,2,128]{3,1,2,0:T(8,128)(2,1)S(1)} %collective-permute-done), kind=kOutput, calls=%fused_computation.6.clone.1 | convolution fusion | flops 612433920 | bytes 3342336 | tf_op jit(solution)/shard_map/while/body/hqk,khd->qhd/dot_general | solution.py:31
  148.3 1.9 collective-permute-start
  150.3 0.6 and_and_fusion.3
  150.9 15.5 %collective-permute-done = bf16[2,768,2,128]{3,1,2,0:T(8,128)(2,1)S(1)} collective-permute-done((bf16[2,768,2,128]{3,1,2,0:T(8,128)(2,1)}, bf16[2,768,2,128]{3,1,2,0:T(8,128)(2,1)S(1)}, u32[]{:S(2)}, u32[]{:S(2)}) %collective-permute-start) | collective-permute-done | bytes 786464 | tf_op jit(solution)/shard_map/while/body/ppermute | solution.py:13
  166.5 0.9 copy.55
  167.4 3.3 %fusion.45 = f32[768,2,128]{2,0,1:T(8,128)S(1)} fusion(f32[768,2,128]{2,0,1:T(8,128)S(1)} %get-tuple-element.347, pred[768,768]{1,0:T(8,128)(4,1)S(1)} %and_and_fusion.3, bf16[768,2,128]{2,0,1:T(8,128)(2,1)} %get-tuple-element.363, bf16[2,768,2,128]{3,1,2,0:T(8,128)(2,1)S(1)} %collective-permute-done), kind=kOutput, calls=%fused_computation.6.clone.1 | convolution fusion | flops 612433920 | bytes 3342336 | tf_op jit(solution)/shard_map/while/body/hqk,khd->qhd/dot_general | solution.py:31
  171.3 1.9 collective-permute-start
  173.4 0.6 and_and_fusion.3
  174.0 14.6 %collective-permute-done = bf16[2,768,2,128]{3,1,2,0:T(8,128)(2,1)S(1)} collective-permute-done((bf16[2,768,2,128]{3,1,2,0:T(8,128)(2,1)}, bf16[2,768,2,128]{3,1,2,0:T(8,128)(2,1)S(1)}, u32[]{:S(2)}, u32[]{:S(2)}) %collective-permute-start) | collective-permute-done | bytes 786464 | tf_op jit(solution)/shard_map/while/body/ppermute | solution.py:13
  188.6 0.9 copy.55
  189.5 3.3 %fusion.45 = f32[768,2,128]{2,0,1:T(8,128)S(1)} fusion(f32[768,2,128]{2,0,1:T(8,128)S(1)} %get-tuple-element.347, pred[768,768]{1,0:T(8,128)(4,1)S(1)} %and_and_fusion.3, bf16[768,2,128]{2,0,1:T(8,128)(2,1)} %get-tuple-element.363, bf16[2,768,2,128]{3,1,2,0:T(8,128)(2,1)S(1)} %collective-permute-done), kind=kOutput, calls=%fused_computation.6.clone.1 | convolution fusion | flops 612433920 | bytes 3342336 | tf_op jit(solution)/shard_map/while/body/hqk,khd->qhd/dot_general | solution.py:31
  193.9 10.7 %psum.7 = f32[768]{0:T(1024)S(1)} all-reduce(f32[768]{0:T(1024)S(1)} %multiply_reduce_fusion), channel_id=1, replica_groups=mesh['ctx'=8,'head'=4] {'head'}, use_global_device_ids=true, to_apply=%region_11.12 | all-reduce | flops 768 | bytes 6144 | tf_op jit(solution)/shard_map/psum | solution.py:91
  205.2 2.3 fusion.37
  207.5 37.4 %reduce-scatter.2.cloned.1.call-done = f32[768,256]{1,0:T(8,128)} async-done(((f32[768,1024]{1,0:T(8,128)}), f32[768,256]{1,0:T(8,128)}) %reduce-scatter.2.cloned.1.call-update) | async-done | bytes 786448 | tf_op jit(solution)/shard_map/reduce_scatter | solution.py:99
  244.9 2.0 add_convert_fusion
  (50 shorter events, 2.7 us)
Async XLA Ops:
  6.5 198.6 %copy-start = (bf16[256,1024]{1,0:T(8,128)(2,1)S(1)}, bf16[256,1024]{1,0:T(8,128)(2,1)}, u32[]{:S(2)}) copy-start(bf16[256,1024]{1,0:T(8,128)(2,1)} %param.10) | copy-start | bytes 1572868
  6.5 2.9 %copy-start.5 = (s32[8]{0:T(128)S(1)}, s32[8]{0:T(128)}, u32[]{:S(2)}) copy-start(s32[8]{0:T(128)} %param.11) | copy-start | bytes 100
  6.5 22.8 %all-gather.2.cloned.1.call-start = ((), (), s32[]{:S(2)}) async-start(), calls=%async_computation.1 | async-start | bytes 1966080 | tf_op jit(solution)/shard_map/all_gather | solution.py:39
  7.3 237.6 %reduce-scatter.2.cloned.1.call-start = ((), (), s32[]{:S(2)}) async-start(), calls=%async_computation.2 | async-start | bytes 3932160 | tf_op jit(solution)/shard_map/reduce_scatter | solution.py:99
  7.3 25.9 %copy-start.4 = (f32[1024]{0:T(1024)S(1)}, f32[1024]{0:T(1024)}, u32[]{:S(2)}) copy-start(f32[1024]{0:T(1024)} %param.8) | copy-start | bytes 12292
  29.4 3.8 %copy-start.1 = (bf16[768,1024]{1,0:T(8,128)(2,1)S(1)}, bf16[768,1024]{1,0:T(8,128)(2,1)}, u32[]{:S(2)}) copy-start(bf16[768,1024]{1,0:T(8,128)(2,1)} %all-gather.2.cloned.1.call-done) | copy-start | bytes 4718596
  40.5 0.9 copy-start.2
  46.9 21.9 %collective-permute-start = (bf16[2,768,2,128]{3,1,2,0:T(8,128)(2,1)}, bf16[2,768,2,128]{3,1,2,0:T(8,128)(2,1)S(1)}, u32[]{:S(2)}, u32[]{:S(2)}) collective-permute-start(bf16[2,768,2,128]{3,1,2,0:T(8,128)(2,1)} %get-tuple-element.348), channel_id=1, source_target_pairs={{0,4},{4,8},{8,12},{12,16},{16,20},{20,24},{24,28},{1,5},{5,9},{9,... | collective-permute-start | bytes 2359304 | tf_op jit(solution)/shard_map/while/body/ppermute | solution.py:13
  73.7 21.0 %collective-permute-start = (bf16[2,768,2,128]{3,1,2,0:T(8,128)(2,1)}, bf16[2,768,2,128]{3,1,2,0:T(8,128)(2,1)S(1)}, u32[]{:S(2)}, u32[]{:S(2)}) collective-permute-start(bf16[2,768,2,128]{3,1,2,0:T(8,128)(2,1)} %get-tuple-element.348), channel_id=1, source_target_pairs={{0,4},{4,8},{8,12},{12,16},{16,20},{20,24},{24,28},{1,5},{5,9},{9,... | collective-permute-start | bytes 2359304 | tf_op jit(solution)/shard_map/while/body/ppermute | solution.py:13
  99.5 20.0 %collective-permute-start = (bf16[2,768,2,128]{3,1,2,0:T(8,128)(2,1)}, bf16[2,768,2,128]{3,1,2,0:T(8,128)(2,1)S(1)}, u32[]{:S(2)}, u32[]{:S(2)}) collective-permute-start(bf16[2,768,2,128]{3,1,2,0:T(8,128)(2,1)} %get-tuple-element.348), channel_id=1, source_target_pairs={{0,4},{4,8},{8,12},{12,16},{16,20},{20,24},{24,28},{1,5},{5,9},{9,... | collective-permute-start | bytes 2359304 | tf_op jit(solution)/shard_map/while/body/ppermute | solution.py:13
  124.3 19.1 %collective-permute-start = (bf16[2,768,2,128]{3,1,2,0:T(8,128)(2,1)}, bf16[2,768,2,128]{3,1,2,0:T(8,128)(2,1)S(1)}, u32[]{:S(2)}, u32[]{:S(2)}) collective-permute-start(bf16[2,768,2,128]{3,1,2,0:T(8,128)(2,1)} %get-tuple-element.348), channel_id=1, source_target_pairs={{0,4},{4,8},{8,12},{12,16},{16,20},{20,24},{24,28},{1,5},{5,9},{9,... | collective-permute-start | bytes 2359304 | tf_op jit(solution)/shard_map/while/body/ppermute | solution.py:13
  148.3 18.2 %collective-permute-start = (bf16[2,768,2,128]{3,1,2,0:T(8,128)(2,1)}, bf16[2,768,2,128]{3,1,2,0:T(8,128)(2,1)S(1)}, u32[]{:S(2)}, u32[]{:S(2)}) collective-permute-start(bf16[2,768,2,128]{3,1,2,0:T(8,128)(2,1)} %get-tuple-element.348), channel_id=1, source_target_pairs={{0,4},{4,8},{8,12},{12,16},{16,20},{20,24},{24,28},{1,5},{5,9},{9,... | collective-permute-start | bytes 2359304 | tf_op jit(solution)/shard_map/while/body/ppermute | solution.py:13
  171.3 17.3 %collective-permute-start = (bf16[2,768,2,128]{3,1,2,0:T(8,128)(2,1)}, bf16[2,768,2,128]{3,1,2,0:T(8,128)(2,1)S(1)}, u32[]{:S(2)}, u32[]{:S(2)}) collective-permute-start(bf16[2,768,2,128]{3,1,2,0:T(8,128)(2,1)} %get-tuple-element.348), channel_id=1, source_target_pairs={{0,4},{4,8},{8,12},{12,16},{16,20},{20,24},{24,28},{1,5},{5,9},{9,... | collective-permute-start | bytes 2359304 | tf_op jit(solution)/shard_map/while/body/ppermute | solution.py:13
  205.2 39.8 %copy-start.3 = (bf16[768,256]{1,0:T(8,128)(2,1)S(1)}, bf16[768,256]{1,0:T(8,128)(2,1)}, u32[]{:S(2)}) copy-start(bf16[768,256]{1,0:T(8,128)(2,1)} %param.7) | copy-start | bytes 1179652
Sparse Core Ops, SparseCore 0:
  8.9 20.4 all-gather.1
  207.6 37.2 reduce-scatter.1
where the time goes:
time: 257 us; the launch traced here: 254 us
  waiting for transfers between devices  156 us (61%)
  matrix products  29.1 us (11%)
  other arithmetic  13.9 us (5%)
  between operations  13.6 us (5%)
  local copies, waits for them, and re-layouts  13.2 us (5%)
  starting transfers between devices  13 us (5%)
  blocking collectives  10.7 us (4%)
  loops' own time  4.77 us (2%)
    ppermute x6, waiting for transfers between devices, passed_along(): return lax.ppermute(value, axis, pairs)  100 us
    reduce_scatter x1, waiting for transfers between devices, shards(): lax.psum_scatter(partial_out, 'head', scatter_dimension=1, tiled=True)  37.4 us
    dot_general x7, matrix products, attend(): jnp.einsum('hqk,khd->qhd', weights, value_block, preferred_element_type=j...  23.4 us
    all_gather x1, waiting for transfers between devices, shards(): gathered = lax.all_gather(events, 'head', axis=1, tiled=True)  17.2 us
    ppermute x6, starting transfers between devices, passed_along(): return lax.ppermute(value, axis, pairs)  13 us
    psum x1, blocking collectives, shards(): squares = lax.psum(local_squares, 'head')  10.7 us
    while x6, local copies, waits for them, and re-layouts  5.26 us
  transfers between devices with their start and end apart: 8, of which 8 were waited for; matrix products, arithmetic and copies ran while one was open for 4% of the time, Pallas kernels for 0%

commit v1 on v0

v1 whole, which is shorter than its diff:
```python
import functools

import jax
import jax.numpy as jnp
from jax import lax
from jax.experimental import pallas as pl
from jax.experimental.pallas import tpu as pltpu
from jax.sharding import PartitionSpec as P

HDIM = 128
EPS = 1e-05
MESH = pl.DeviceIdType.MESH
F32 = jnp.float32
BF16 = jnp.bfloat16


def silu(z):
    t = 0.5 * z
    return t + t * jnp.tanh(t)


def kernel(
    line, ev, gain, w, wout, lengths, out,
    xall, nbuf, kbuf, vbuf, gate, qbuf, resf, res_in, res_out, att, gs, go, sqs, sqall, wall,
    sA, rA, qs, qr, rs, rr, sE, rE, ws, wr, ss, sr,
):
    T, F = ev.shape
    D = xall.shape[1]
    C = T // 2
    SLAB = 2 * T
    NC = 4
    KT = 256 if SLAB % 256 == 0 else C
    c = lax.axis_index("ctx")
    h = lax.axis_index("head")
    x = c % 2
    ox = 1 - x
    zz = c // 2
    sh = h + 1 - 2 * (h % 2)
    yh = (h + 2) % 4
    me = (c, h)
    sib = (c, sh)
    yn = (c, yh)
    xc = c + 1 - 2 * x
    xn = (xc, h)
    prv = (c - 2, h)
    nxt = (c + 2, h)
    hasp = zz > 0
    hasn = zz < line - 1
    peers = [(c if dx == 0 else xc, (h + dh) % 4, dx, dh) for dx in (0, 1) for dh in range(4) if dx + dh > 0]

    def rc(src, dst, ssem, rsem, dev):
        return pltpu.make_async_remote_copy(
            src_ref=src, dst_ref=dst, send_sem=ssem, recv_sem=rsem, device_id=dev, device_id_type=MESH
        )

    bar = pltpu.get_barrier_semaphore()
    for pc, ph, _, _ in peers:
        pl.semaphore_signal(bar, inc=1, device_id=(pc, ph), device_id_type=MESH)

    @pl.when(hasp)
    def _():
        pl.semaphore_signal(bar, inc=1, device_id=prv, device_id_type=MESH)

    @pl.when(hasn)
    def _():
        pl.semaphore_signal(bar, inc=1, device_id=nxt, device_id_type=MESH)

    pl.semaphore_wait(bar, 7 + hasp.astype(jnp.int32) + hasn.astype(jnp.int32))

    def al(v, m):
        return pl.multiple_of(v, m)

    def piece(g, r, hh):
        return xall.at[pl.ds(al(g * T + r * C, C), C), pl.ds(al(hh * F, F), F)]

    def own_copy(r, slot, kind, dev):
        return rc(ev.at[pl.ds(r * C, C)], piece(x, r, h), sA.at[slot, r], rA.at[kind, r], dev)

    def relay(g, r, hh, slot, kind, dev):
        p = piece(g, r, hh)
        return rc(p, p, sA.at[slot, r], rA.at[kind, r], dev)

    def got(g, r, hh, kind):
        p = piece(g, r, hh)
        rc(p, p, sA.at[0, r], rA.at[kind, r], sib).wait_recv()

    sendsA = []

    def go_send(d):
        d.start()
        sendsA.append(d)

    for r in (0, 1):
        go_send(own_copy(r, 1, 4, yn))
        go_send(own_copy(r, 2, 5, xn))
        go_send(own_copy(r, 0, 0, sib))
    xall[pl.ds(al(x * T, T), T), pl.ds(al(h * F, F), F)] = ev[...]

    def chunk_base(i):
        r = i % 2
        g = jnp.where(i < 2, x, ox)
        return al(g * T + r * C, C)

    LN = 64 if C % 64 == 0 else C

    def qcopy(s, i, dev):
        rows = pl.ds(chunk_base(i), C)
        return rc(qbuf.at[s, rows], qbuf.at[s, rows], qs.at[s, i], qr.at[s, i], dev)

    def project(i):
        base = chunk_base(i)

        def ln(k, carry):
            rows = pl.ds(al(base + k * LN, LN), LN)
            xf = xall[rows, :].astype(F32)
            mean = jnp.mean(xf, axis=-1, keepdims=True)
            cen = xf - mean
            var = jnp.mean(cen * cen, axis=-1, keepdims=True)
            nbuf[pl.ds(al(k * LN, LN), LN), :] = (cen * lax.rsqrt(var + EPS) * gain[...]).astype(BF16)
            return carry

        lax.fori_loop(0, C // LN, ln, 0)
        rows = pl.ds(base, C)
        for half in (1, 0):
            p = silu(
                jnp.dot(nbuf[...], w[:, half * 2 * HDIM:(half + 1) * 2 * HDIM], preferred_element_type=F32)
            ).astype(BF16)
            if half == 1:
                qbuf[zz, rows, :] = p[:, :HDIM]
                kbuf[rows, :] = p[:, HDIM:]

                @pl.when(hasp)
                def _():
                    qcopy(zz, i, prv).start()
            else:
                gate[rows, :] = p[:, :HDIM]
                vbuf[rows, :] = p[:, HDIM:]

    h3 = sh + 2 - 4 * (sh // 2)
    got(x, 0, yh, 4)
    go_send(relay(x, 0, yh, 3, 1, sib))
    got(ox, 0, h, 5)
    go_send(relay(ox, 0, h, 6, 6, yn))
    go_send(relay(ox, 0, h, 4, 2, sib))
    got(x, 0, sh, 0)
    got(x, 0, h3, 1)
    project(0)
    got(x, 1, yh, 4)
    go_send(relay(x, 1, yh, 6, 6, xn))
    go_send(relay(x, 1, yh, 3, 1, sib))
    got(ox, 1, h, 5)
    go_send(relay(ox, 1, h, 4, 2, sib))
    got(x, 1, sh, 0)
    got(x, 1, h3, 1)
    project(1)
    for r in (0, 1):
        got(ox, r, yh, 6)
        go_send(relay(ox, r, yh, 5, 3, sib))
    for dh in (1, 2, 3):
        ph = (h + dh) % 4
        go_send(
            rc(wout.at[:, pl.ds(al(ph * F, F), F)], wall.at[pl.ds(al(h * F, F), F)],
               ws.at[dh - 1], wr.at[dh - 1], (c, ph))
        )
    wall[pl.ds(al(h * F, F), F), :] = wout[:, pl.ds(al(h * F, F), F)]
    for r in (0, 1):
        got(ox, r, sh, 2)
        got(ox, r, h3, 3)
        project(2 + r)

    half_scale = 0.5 * HDIM ** (-0.5)

    def starts_of(first):
        pos = first + lax.broadcasted_iota(jnp.int32, (C, 1), 0)
        end = jnp.int32(0)
        start = jnp.zeros((C, 1), jnp.int32)
        for s in range(lengths.shape[0]):
            end = end + lengths[s]
            start = jnp.where(pos >= end, end, start)
        return pos, start

    def tile_sum(q, start, pos, k0):
        rows = pl.ds(k0, KT)
        t = lax.dot_general(q, kbuf[rows, :], (((1,), (1,)), ((), ())), preferred_element_type=F32) * half_scale
        wgt = t + t * jnp.tanh(t)
        kpos = zz * SLAB + k0 + lax.broadcasted_iota(jnp.int32, (1, KT), 1)
        allowed = kpos >= start
        if pos is not None:
            allowed = allowed & (kpos <= pos)
        wgt = jnp.where(allowed, wgt, 0.0).astype(BF16)
        return jnp.dot(wgt, vbuf[rows, :], preferred_element_type=F32)

    def rcopy(s, i, dev):
        rows = pl.ds(chunk_base(i), C)
        return rc(res_out.at[s, rows], res_in.at[s, rows], rs.at[s, i], rr.at[s, i], dev)

    def incoming(t, carry):
        s = zz + 1 + t // NC
        i = t % NC
        base = chunk_base(i)
        qcopy(s, i, prv).wait_recv()

        @pl.when(hasp)
        def _():
            qcopy(s, i, prv).start()

        rows = pl.ds(base, C)
        q = qbuf[s, rows, :]
        _, start = starts_of(s * SLAB + base)
        total = jnp.zeros((C, HDIM), F32)
        for k in range(SLAB // KT):
            total = total + tile_sum(q, start, None, k * KT)

        @pl.when(hasp)
        def _():
            resf[s, rows, :] = total

        @pl.when(zz == 0)
        def _():
            res_out[s, rows, :] = total.astype(BF16)
            rcopy(s, i, nxt).start()

        return carry

    items = NC * (line - 1 - zz)
    lax.fori_loop(0, items, incoming, 0)

    def diagonal(i, carry):
        base = chunk_base(i)
        rows = pl.ds(base, C)
        q = qbuf[zz, rows, :]
        pos, start = starts_of(zz * SLAB + base)
        att[rows, :] = jnp.zeros((C, HDIM), F32)

        def one(k, carry):
            att[rows, :] += tile_sum(q, start, pos, al(k * KT, KT))
            return carry

        lax.fori_loop(0, (base + C + KT - 1) // KT, one, 0)
        return carry

    lax.fori_loop(0, NC, diagonal, 0)

    @pl.when(hasp)
    def _():
        def onward(t, carry):
            s = zz + 1 + t // NC
            i = t % NC
            rows = pl.ds(chunk_base(i), C)
            rcopy(s, i, nxt).wait_recv()
            res_out[s, rows, :] = (resf[s, rows, :] + res_in[s, rows, :].astype(F32)).astype(BF16)
            rcopy(s, i, nxt).start()
            return carry

        lax.fori_loop(0, items, onward, 0)

    def epiece(xs, r, hs):
        return go.at[pl.ds(r * C, C), pl.ds(al(hs * F + xs * HDIM, HDIM), HDIM)]

    def erelay(xs, r, hs, slot, kind, dev):
        p = epiece(xs, r, hs)
        return rc(p, p, sE.at[slot, r], rE.at[kind, r], dev)

    def egot(xs, r, hs, kind):
        p = epiece(xs, r, hs)
        rc(p, p, sE.at[0, r], rE.at[kind, r], sib).wait_recv()

    ones = jnp.ones((8, HDIM), BF16)
    for i in range(NC):
        r = i % 2
        base = chunk_base(jnp.int32(i))
        rows = pl.ds(base, C)

        @pl.when(hasp)
        def _():
            rcopy(zz, i, nxt).wait_recv()
            att[rows, :] += res_in[zz, rows, :].astype(F32)

        a = att[rows, :]
        gs[rows, :] = (a * gate[rows, :].astype(F32)).astype(BF16)
        src = gs.at[rows]
        if i < 2:
            go_send(rc(src, epiece(x, r, h), sE.at[1, r], rE.at[4, r], yn))
            go_send(rc(src, epiece(x, r, h), sE.at[0, r], rE.at[0, r], sib))
            go[r * C:(r + 1) * C, pl.ds(al(h * F + x * HDIM, HDIM), HDIM)] = gs[rows, :]
        else:
            go_send(rc(src, epiece(x, r, h), sE.at[2, r], rE.at[5, r], xn))
        sq = a * a
        hi = sq.astype(BF16)
        lo = (sq - hi.astype(F32)).astype(BF16)
        dims = (((1,), (1,)), ((), ()))
        sqs[:, pl.ds(base, C)] = lax.dot_general(ones, hi, dims, preferred_element_type=F32) + lax.dot_general(
            ones, lo, dims, preferred_element_type=F32
        )
    for n, (pc, ph, dx, dh) in enumerate(peers):
        grp = x if dx == 0 else ox
        go_send(rc(sqs.at[:, pl.ds(al(grp * T, T), T)], sqall.at[n], ss.at[n], sr.at[n], (pc, ph)))
    for r in (0, 1):
        egot(x, r, yh, 4)
        go_send(erelay(x, r, yh, 3, 1, sib))
    for r in (0, 1):
        egot(ox, r, h, 5)
        go_send(erelay(ox, r, h, 6, 6, yn))
        go_send(erelay(ox, r, h, 4, 2, sib))
    for dh in (1, 2, 3):
        src_h = (h + 4 - dh) % 4
        rc(wout.at[:, pl.ds(0, F)], wall.at[pl.ds(al(src_h * F, F), F)], ws.at[dh - 1], wr.at[dh - 1], sib).wait_recv()
    squares = sqs[:, pl.ds(al(x * T, T), T)]
    for n in range(7):
        rc(sqs.at[:, pl.ds(0, T)], sqall.at[n], ss.at[n], sr.at[n], sib).wait_recv()
        squares = squares + sqall[n]
    inv = lax.rsqrt(squares / D + EPS)
    inv = jnp.broadcast_to(inv[0:1], (HDIM, T)).T
    for r in (0, 1):
        egot(ox, r, yh, 6)
        go_send(erelay(ox, r, yh, 5, 3, sib))
    for r in (0, 1):
        egot(x, r, sh, 0)
        egot(x, r, h3, 1)
        egot(ox, r, sh, 2)
        egot(ox, r, h3, 3)
        rows = slice(r * C, (r + 1) * C)
        prod = jnp.dot(go[rows, :], wall[...], preferred_element_type=F32)
        scale = inv[rows, :]
        for k in range(F // HDIM):
            cols = slice(k * HDIM, (k + 1) * HDIM)
            out[rows, cols] = (ev[rows, cols].astype(F32) + prod[:, cols] * scale).astype(BF16)

    for d in sendsA:
        d.wait_send()

    @pl.when(hasp)
    def _():
        def fin(t, carry):
            qcopy(zz + t // NC, t % NC, prv).wait_send()
            return carry

        lax.fori_loop(0, items + NC, fin, 0)

    def fin2(t, carry):
        rcopy(zz + 1 + t // NC, t % NC, nxt).wait_send()
        return carry

    lax.fori_loop(0, items, fin2, 0)


def shards(events, norm_gain, w_uvqk, w_out, lengths):
    T, F = events.shape
    D = w_uvqk.shape[0]
    line = lax.axis_size("ctx") // 2
    x = lax.axis_index("ctx") % 2
    w = lax.dynamic_slice_in_dim(w_uvqk, x * HDIM, HDIM, 2).reshape(D, 4 * HDIM)
    S = 2 * T
    vm = pltpu.VMEM
    dma = pltpu.SemaphoreType.DMA
    vspec = pl.BlockSpec(memory_space=pltpu.VMEM)
    return pl.pallas_call(
        functools.partial(kernel, line),
        out_shape=jax.ShapeDtypeStruct((T, F), BF16),
        in_specs=[vspec] * 4 + [pl.BlockSpec(memory_space=pltpu.SMEM)],
        out_specs=vspec,
        scratch_shapes=[
            vm((S, D), BF16), vm((T // 2, D), BF16), vm((S, HDIM), BF16), vm((S, HDIM), BF16), vm((S, HDIM), BF16),
            vm((line, S, HDIM), BF16), vm((line, S, HDIM), F32), vm((line, S, HDIM), BF16),
            vm((line, S, HDIM), BF16), vm((S, HDIM), F32), vm((S, HDIM), BF16), vm((T, D), BF16),
            vm((8, S), F32), vm((7, 8, T), F32), vm((D, F), BF16),
            dma((7, 2)), dma((7, 2)), dma((line, 4)), dma((line, 4)), dma((line, 4)), dma((line, 4)),
            dma((7, 2)), dma((7, 2)), dma((3,)), dma((3,)), dma((7,)), dma((7,)),
        ],
        compiler_params=pltpu.CompilerParams(
            collective_id=0, has_side_effects=True, vmem_limit_bytes=56 * 1024 * 1024
        ),
    )(events, norm_gain.reshape(1, D), w, w_out, lengths)


def solution(mesh):
    in_specs = (P("ctx", "head"), P(), P(None, None, "head"), P("head", None), P())
    return jax.shard_map(shards, mesh=mesh, in_specs=in_specs, out_specs=P("ctx", "head"), check_vma=False)
```

time: 257 us -> 84.2 us (0.33); the launches traced: 254 us -> 84 us
  waiting for transfers between devices: 156 us -> 0 us
  Pallas kernels: 0 us -> 79.1 us
  matrix products: 29.1 us -> 0 us
  other arithmetic: 13.9 us -> 0 us
  between operations: 13.6 us -> 0.01 us
  starting transfers between devices: 13 us -> 0 us
  blocking collectives: 10.7 us -> 0 us
  local copies, waits for them, and re-layouts: 13.2 us -> 4.89 us
  loops' own time: 4.77 us -> 0 us
    ppermute x6 -> x0, waiting for transfers between devices: 100 us -> none  [passed_along(): return lax.ppermute(value, axis, pairs)]
    pallas_call x0 -> x1, Pallas kernels: none -> 79.1 us  [shards(): pl.pallas_call(functools.partial(kernel, line), out_shape=jax.ShapeDtypeS...]
    reduce_scatter x1 -> x0, waiting for transfers between devices: 37.4 us -> none  [shards(): lax.psum_scatter(partial_out, 'head', scatter_dimension=1, tiled=True)]
    dot_general x9 -> x0, matrix products: 29.1 us -> none  [the longest x7 23.4 us: attend(): jnp.einsum('hqk,khd->qhd', weights, value_block, preferred_element_type=j...]
    all_gather x1 -> x0, waiting for transfers between devices: 17.2 us -> none  [shards(): gathered = lax.all_gather(events, 'head', axis=1, tiled=True)]
    ppermute x6 -> x0, starting transfers between devices: 13 us -> none  [passed_along(): return lax.ppermute(value, axis, pairs)]
    psum x1 -> x0, blocking collectives: 10.7 us -> none  [shards(): squares = lax.psum(local_squares, 'head')]
    while x7 -> x0, local copies, waits for them, and re-layouts: 5.52 us -> none
  transfers between devices with their start and end apart: 8 -> 0, of which waited for: 8 -> 0; matrix products, arithmetic and copies ran while one was open for 4% -> 0% of each run, Pallas kernels for 0% -> 0%
where the time goes in v1:
time: 84.2 us; the launch traced here: 84 us
  Pallas kernels  79.1 us (94%)
  local copies, waits for them, and re-layouts  4.89 us (6%)
    pallas_call x1, Pallas kernels, shards(): pl.pallas_call(functools.partial(kernel, line), out_shape=jax.ShapeDtypeS...  79.1 us
    unnamed x4, local copies, waits for them, and re-layouts  4.53 us

profile of v1, /device:TPU:21, one launch (start us, length us, event | category | flops | bytes accessed | tf_op | source)
XLA Modules:
  0.0 84.0 jit_solution(11265202130561329868)
XLA Ops:
  0.0 0.0 copy-start
  0.0 1.6 %copy-done = bf16[1024,4,256]{2,1,0:T(4,128)(2,1)S(1)} copy-done((bf16[1024,4,256]{2,1,0:T(4,128)(2,1)S(1)}, bf16[1024,4,256]{2,1,0:T(4,128)(2,1)}, u32[]{:S(2)}) %copy-start) | copy-done | bytes 2097176
  1.6 0.4 constant_dynamic-slice_fusion
  2.0 1.2 %copy.8 = bf16[128,8,4,128]{3,1,2,0:T(8,128)(2,1)} copy(bf16[128,8,4,128]{3,2,1,0:T(4,128)(2,1)S(1)} %bitcast.5) | data formatting | bytes 2097152
  3.1 79.1 %shard_map.55 = bf16[768,256]{1,0:T(8,128)(2,1)} custom-call(bf16[768,256]{1,0:T(8,128)(2,1)} %ev.1, f32[1,1024]{1,0:T(1,128)} %bitcast.7, bf16[1024,512]{1,0:T(8,128)(2,1)} %bitcast.6, bf16[256,1024]{1,0:T(8,128)(2,1)} %wout.1, s32[8]{0:T(128)} %lengths.1), custom_call_target="tpu_custom_call" | custom-call | tf_op jit(solution)/shard_map/pallas_call | solution.py:357
  82.2 1.8 %copy.10 = bf16[768,256]{1,0:T(8,128)(2,1)} copy(bf16[768,256]{1,0:T(8,128)(2,1)} %shard_map.55) | data formatting | bytes 786432
Async XLA Ops:
  0.0 1.6 %copy-start = (bf16[1024,4,256]{2,1,0:T(4,128)(2,1)S(1)}, bf16[1024,4,256]{2,1,0:T(4,128)(2,1)}, u32[]{:S(2)}) copy-start(bf16[1024,4,256]{2,1,0:T(4,128)(2,1)} %param.7) | copy-start | bytes 6291460

commit v2 on v1

--- a/solution.py
+++ b/solution.py
@@ -21,7 +21,7 @@
 
 def kernel(
     line, ev, gain, w, wout, lengths, out,
-    xall, nbuf, kbuf, vbuf, gate, qbuf, resf, res_in, res_out, att, gs, go, sqs, sqall, wall,
+    xall, nbuf, kbuf, wgt_buf, vbuf, gate, qbuf, resf, res_in, res_out, att, gs, go, sqs, sqall, wall,
     sA, rA, qs, qr, rs, rr, sE, rE, ws, wr, ss, sr,
 ):
     T, F = ev.shape
@@ -101,6 +101,7 @@
         g = jnp.where(i < 2, x, ox)
         return al(g * T + r * C, C)
 
+    RB = 128 if C % 128 == 0 else C
     LN = 64 if C % 64 == 0 else C
 
     def qcopy(s, i, dev):
@@ -127,7 +128,7 @@
             ).astype(BF16)
             if half == 1:
                 qbuf[zz, rows, :] = p[:, :HDIM]
-                kbuf[rows, :] = p[:, HDIM:]
+                kbuf[:, rows] = p[:, HDIM:].astype(F32).T.astype(BF16)
 
                 @pl.when(hasp)
                 def _():
@@ -179,16 +180,17 @@
             start = jnp.where(pos >= end, end, start)
         return pos, start
 
-    def tile_sum(q, start, pos, k0):
-        rows = pl.ds(k0, KT)
-        t = lax.dot_general(q, kbuf[rows, :], (((1,), (1,)), ((), ())), preferred_element_type=F32) * half_scale
+    def tile_weights(q, start, pos, k0):
+        t = jnp.dot(q, kbuf[:, pl.ds(k0, KT)], preferred_element_type=F32) * half_scale
         wgt = t + t * jnp.tanh(t)
         kpos = zz * SLAB + k0 + lax.broadcasted_iota(jnp.int32, (1, KT), 1)
         allowed = kpos >= start
         if pos is not None:
             allowed = allowed & (kpos <= pos)
-        wgt = jnp.where(allowed, wgt, 0.0).astype(BF16)
-        return jnp.dot(wgt, vbuf[rows, :], preferred_element_type=F32)
+        return jnp.where(allowed, wgt, 0.0).astype(BF16)
+
+    def tile_sum(q, start, pos, k0):
+        return jnp.dot(tile_weights(q, start, pos, k0), vbuf[pl.ds(k0, KT), :], preferred_element_type=F32)
 
     def rcopy(s, i, dev):
         rows = pl.ds(chunk_base(i), C)
@@ -207,9 +209,13 @@
         rows = pl.ds(base, C)
         q = qbuf[s, rows, :]
         _, start = starts_of(s * SLAB + base)
-        total = jnp.zeros((C, HDIM), F32)
-        for k in range(SLAB // KT):
-            total = total + tile_sum(q, start, None, k * KT)
+        parts = []
+        for b in range(C // RB):
+            blk = slice(b * RB, (b + 1) * RB)
+            for k in range(SLAB // KT):
+                wgt_buf[blk, k * KT:(k + 1) * KT] = tile_weights(q[blk], start[blk], None, k * KT)
+            parts.append(jnp.dot(wgt_buf[blk, :], vbuf[...], preferred_element_type=F32))
+        total = jnp.concatenate(parts, axis=0)
 
         @pl.when(hasp)
         def _():
@@ -324,7 +330,7 @@
         scale = inv[rows, :]
         for k in range(F // HDIM):
             cols = slice(k * HDIM, (k + 1) * HDIM)
-            out[rows, cols] = (ev[rows, cols].astype(F32) + prod[:, cols] * scale).astype(BF16)
+            out[rows, cols] = prod[:, cols] * scale
 
     for d in sendsA:
         d.wait_send()
@@ -354,13 +360,14 @@
     vm = pltpu.VMEM
     dma = pltpu.SemaphoreType.DMA
     vspec = pl.BlockSpec(memory_space=pltpu.VMEM)
-    return pl.pallas_call(
+    delta = pl.pallas_call(
         functools.partial(kernel, line),
-        out_shape=jax.ShapeDtypeStruct((T, F), BF16),
+        out_shape=jax.ShapeDtypeStruct((T, F), F32),
         in_specs=[vspec] * 4 + [pl.BlockSpec(memory_space=pltpu.SMEM)],
         out_specs=vspec,
         scratch_shapes=[
-            vm((S, D), BF16), vm((T // 2, D), BF16), vm((S, HDIM), BF16), vm((S, HDIM), BF16), vm((S, HDIM), BF16),
+            vm((S, D), BF16), vm((T // 2, D), BF16), vm((HDIM, S), BF16), vm((T // 2, S), BF16), vm((S, HDIM), BF16),
+            vm((S, HDIM), BF16),
             vm((line, S, HDIM), BF16), vm((line, S, HDIM), F32), vm((line, S, HDIM), BF16),
             vm((line, S, HDIM), BF16), vm((S, HDIM), F32), vm((S, HDIM), BF16), vm((T, D), BF16),
             vm((8, S), F32), vm((7, 8, T), F32), vm((D, F), BF16),
@@ -371,6 +378,7 @@
             collective_id=0, has_side_effects=True, vmem_limit_bytes=56 * 1024 * 1024
         ),
     )(events, norm_gain.reshape(1, D), w, w_out, lengths)
+    return (events.astype(F32) + delta).astype(BF16)
 
 
 def solution(mesh):

time: 84.2 us -> 84.3 us (level)
  other arithmetic: 0 us -> 1.96 us
  local copies, waits for them, and re-layouts: 4.89 us -> 3.12 us
    convert_element_type x0 -> x1, other arithmetic: none -> 1.96 us  [shards(): return (events.astype(F32) + delta).astype(BF16)]
    unnamed x4 -> x5, local copies, waits for them, and re-layouts: 4.53 us -> 2.76 us
where the time goes in v2:
time: 84.3 us; the launch traced here: 84.1 us
  Pallas kernels  79 us (94%)
  local copies, waits for them, and re-layouts  3.12 us (4%)
  other arithmetic  1.96 us (2%)
    pallas_call x1, Pallas kernels, shards(): pl.pallas_call(functools.partial(kernel, line), out_shape=jax.ShapeDtypeS...  79 us
    unnamed x5, local copies, waits for them, and re-layouts  2.76 us
    convert_element_type x1, other arithmetic, shards(): return (events.astype(F32) + delta).astype(BF16)  1.96 us

profile of v2, /device:TPU:21, one launch (start us, length us, event | category | flops | bytes accessed | tf_op | source)
XLA Modules:
  0.0 84.1 jit_solution(10826100872468364017)
XLA Ops:
  0.0 0.0 copy-start
  0.0 1.6 %copy-done = bf16[1024,4,256]{2,1,0:T(4,128)(2,1)S(1)} copy-done((bf16[1024,4,256]{2,1,0:T(4,128)(2,1)S(1)}, bf16[1024,4,256]{2,1,0:T(4,128)(2,1)}, u32[]{:S(2)}) %copy-start) | copy-done | bytes 2097176
  1.6 0.4 constant_dynamic-slice_fusion
  2.0 0.0 copy-start.1
  2.0 1.2 %copy.8 = bf16[128,8,4,128]{3,1,2,0:T(8,128)(2,1)} copy(bf16[128,8,4,128]{3,2,1,0:T(4,128)(2,1)S(1)} %bitcast.5) | data formatting | bytes 2097152
  3.1 79.0 %shard_map.55 = f32[768,256]{1,0:T(8,128)} custom-call(bf16[768,256]{1,0:T(8,128)(2,1)} %ev.1, f32[1,1024]{1,0:T(1,128)} %bitcast.7, bf16[1024,512]{1,0:T(8,128)(2,1)} %bitcast.6, bf16[256,1024]{1,0:T(8,128)(2,1)} %wout.1, s32[8]{0:T(128)} %lengths.1), custom_call_target="tpu_custom_call" | custom-call | tf_op jit(solution)/shard_map/pallas_call | solution.py:363
  82.1 0.0 copy-done.1
  82.1 2.0 %add_convert_fusion = bf16[768,256]{1,0:T(8,128)(2,1)} fusion(f32[768,256]{1,0:T(8,128)} %shard_map.55, bf16[768,256]{1,0:T(8,128)(2,1)S(1)} %copy-done.1), kind=kLoop, calls=%fused_computation.1 | loop fusion | flops 589824 | bytes 1572864 | tf_op jit(solution)/shard_map/convert_element_type | solution.py:381
Async XLA Ops:
  0.0 1.6 %copy-start = (bf16[1024,4,256]{2,1,0:T(4,128)(2,1)S(1)}, bf16[1024,4,256]{2,1,0:T(4,128)(2,1)}, u32[]{:S(2)}) copy-start(bf16[1024,4,256]{2,1,0:T(4,128)(2,1)} %param.7) | copy-start | bytes 6291460
  2.0 80.2 %copy-start.1 = (bf16[768,256]{1,0:T(8,128)(2,1)S(1)}, bf16[768,256]{1,0:T(8,128)(2,1)}, u32[]{:S(2)}) copy-start(bf16[768,256]{1,0:T(8,128)(2,1)} %ev.1) | copy-start | bytes 1179652

commit v3 on v1

--- a/solution.py
+++ b/solution.py
@@ -21,8 +21,8 @@
 
 def kernel(
     line, ev, gain, w, wout, lengths, out,
-    xall, nbuf, kbuf, vbuf, gate, qbuf, resf, res_in, res_out, att, gs, go, sqs, sqall, wall,
-    sA, rA, qs, qr, rs, rr, sE, rE, ws, wr, ss, sr,
+    xall, nbuf, kbuf, wgt_buf, vbuf, kprev, vprev, gate, qbuf, resf, res_in, res_out, att, gs, go, sqs, sqall, wall,
+    sA, rA, qs, qr, rs, rr, sE, rE, ws, wr, ss, sr, ks, kr, vs, vr,
 ):
     T, F = ev.shape
     D = xall.shape[1]
@@ -101,11 +101,20 @@
         g = jnp.where(i < 2, x, ox)
         return al(g * T + r * C, C)
 
+    RB = 128 if C % 128 == 0 else C
     LN = 64 if C % 64 == 0 else C
 
     def qcopy(s, i, dev):
         rows = pl.ds(chunk_base(i), C)
         return rc(qbuf.at[s, rows], qbuf.at[s, rows], qs.at[s, i], qr.at[s, i], dev)
+
+    def kcopy(i):
+        cols = pl.ds(chunk_base(i), C)
+        return rc(kbuf.at[:, cols], kprev.at[:, cols], ks.at[i], kr.at[i], nxt)
+
+    def vcopy(i):
+        rows = pl.ds(chunk_base(i), C)
+        return rc(vbuf.at[rows], vprev.at[rows], vs.at[i], vr.at[i], nxt)
 
     def project(i):
         base = chunk_base(i)
@@ -127,14 +136,22 @@
             ).astype(BF16)
             if half == 1:
                 qbuf[zz, rows, :] = p[:, :HDIM]
-                kbuf[rows, :] = p[:, HDIM:]
-
-                @pl.when(hasp)
+                kbuf[:, rows] = p[:, HDIM:].astype(F32).T.astype(BF16)
+
+                @pl.when(zz > 1)
                 def _():
                     qcopy(zz, i, prv).start()
+
+                @pl.when(hasn)
+                def _():
+                    kcopy(i).start()
             else:
                 gate[rows, :] = p[:, :HDIM]
                 vbuf[rows, :] = p[:, HDIM:]
+
+                @pl.when(hasn)
+                def _():
+                    vcopy(i).start()
 
     h3 = sh + 2 - 4 * (sh // 2)
     got(x, 0, yh, 4)
@@ -179,51 +196,23 @@
             start = jnp.where(pos >= end, end, start)
         return pos, start
 
-    def tile_sum(q, start, pos, k0):
-        rows = pl.ds(k0, KT)
-        t = lax.dot_general(q, kbuf[rows, :], (((1,), (1,)), ((), ())), preferred_element_type=F32) * half_scale
+    def tile_weights(q, start, pos, k0, keys, first):
+        t = jnp.dot(q, keys[:, pl.ds(k0, KT)], preferred_element_type=F32) * half_scale
         wgt = t + t * jnp.tanh(t)
-        kpos = zz * SLAB + k0 + lax.broadcasted_iota(jnp.int32, (1, KT), 1)
+        kpos = first + k0 + lax.broadcasted_iota(jnp.int32, (1, KT), 1)
         allowed = kpos >= start
         if pos is not None:
             allowed = allowed & (kpos <= pos)
-        wgt = jnp.where(allowed, wgt, 0.0).astype(BF16)
-        return jnp.dot(wgt, vbuf[rows, :], preferred_element_type=F32)
-
-    def rcopy(s, i, dev):
-        rows = pl.ds(chunk_base(i), C)
-        return rc(res_out.at[s, rows], res_in.at[s, rows], rs.at[s, i], rr.at[s, i], dev)
-
-    def incoming(t, carry):
-        s = zz + 1 + t // NC
-        i = t % NC
-        base = chunk_base(i)
-        qcopy(s, i, prv).wait_recv()
-
-        @pl.when(hasp)
-        def _():
-            qcopy(s, i, prv).start()
-
-        rows = pl.ds(base, C)
-        q = qbuf[s, rows, :]
-        _, start = starts_of(s * SLAB + base)
-        total = jnp.zeros((C, HDIM), F32)
-        for k in range(SLAB // KT):
-            total = total + tile_sum(q, start, None, k * KT)
-
-        @pl.when(hasp)
-        def _():
-            resf[s, rows, :] = total
-
-        @pl.when(zz == 0)
-        def _():
-            res_out[s, rows, :] = total.astype(BF16)
-            rcopy(s, i, nxt).start()
-
-        return carry
-
-    items = NC * (line - 1 - zz)
-    lax.fori_loop(0, items, incoming, 0)
+        return jnp.where(allowed, wgt, 0.0).astype(BF16)
+
+    def whole_slab(q, start, keys, values, first):
+        parts = []
+        for b in range(C // RB):
+            blk = slice(b * RB, (b + 1) * RB)
+            for k in range(SLAB // KT):
+                wgt_buf[blk, k * KT:(k + 1) * KT] = tile_weights(q[blk], start[blk], None, k * KT, keys, first)
+            parts.append(jnp.dot(wgt_buf[blk, :], values[...], preferred_element_type=F32))
+        return jnp.concatenate(parts, axis=0)
 
     def diagonal(i, carry):
         base = chunk_base(i)
@@ -233,18 +222,92 @@
         att[rows, :] = jnp.zeros((C, HDIM), F32)
 
         def one(k, carry):
-            att[rows, :] += tile_sum(q, start, pos, al(k * KT, KT))
+            k0 = al(k * KT, KT)
+            wgt = tile_weights(q, start, pos, k0, kbuf, zz * SLAB)
+            att[rows, :] += jnp.dot(wgt, vbuf[pl.ds(k0, KT), :], preferred_element_type=F32)
             return carry
 
         lax.fori_loop(0, (base + C + KT - 1) // KT, one, 0)
         return carry
 
-    lax.fori_loop(0, NC, diagonal, 0)
+    @pl.when(zz == 0)
+    def _():
+        lax.fori_loop(0, NC, diagonal, 0)
+
+    def rcopy(s, i, dev):
+        rows = pl.ds(chunk_base(i), C)
+        return rc(res_out.at[s, rows], res_in.at[s, rows], rs.at[s, i], rr.at[s, i], dev)
+
+    def passing(i, carry):
+        qcopy(zz + 1, i, prv).wait_recv()
+        qcopy(zz + 1, i, prv).start()
+        return carry
+
+    @pl.when(hasp & hasn)
+    def _():
+        lax.fori_loop(0, NC, passing, 0)
+
+    def incoming(t, carry):
+        s = zz + 2 + t // NC
+        i = t % NC
+        base = chunk_base(i)
+        qcopy(s, i, prv).wait_recv()
+
+        @pl.when(hasp)
+        def _():
+            qcopy(s, i, prv).start()
+
+        rows = pl.ds(base, C)
+        q = qbuf[s, rows, :]
+        _, start = starts_of(s * SLAB + base)
+        total = whole_slab(q, start, kbuf, vbuf, zz * SLAB)
+
+        @pl.when(hasp)
+        def _():
+            resf[s, rows, :] = total
+
+        @pl.when(zz == 0)
+        def _():
+            res_out[s, rows, :] = total.astype(BF16)
+            rcopy(s, i, nxt).start()
+
+        return carry
+
+    items = jnp.where(zz < line - 2, NC * (line - 2 - zz), 0)
+    lax.fori_loop(0, items, incoming, 0)
 
     @pl.when(hasp)
     def _():
+        lax.fori_loop(0, NC, diagonal, 0)
+
+        for i in range(NC):
+            kcopy(i).wait_recv()
+            vcopy(i).wait_recv()
+
+        def crossing(i, carry):
+            base = chunk_base(i)
+            rows = pl.ds(base, C)
+            _, start = starts_of(zz * SLAB + base)
+            att[rows, :] += whole_slab(qbuf[zz, rows, :], start, kprev, vprev, (zz - 1) * SLAB)
+            return carry
+
+        lax.fori_loop(0, NC, crossing, 0)
+
+    def pass_on(s, i):
+        rows = pl.ds(chunk_base(i), C)
+        return rc(res_in.at[s, rows], res_in.at[s, rows], rs.at[s, i], rr.at[s, i], nxt)
+
+    @pl.when(hasp & hasn)
+    def _():
+        def straight(i, carry):
+            rcopy(zz + 1, i, nxt).wait_recv()
+            pass_on(zz + 1, i).start()
+            return carry
+
+        lax.fori_loop(0, NC, straight, 0)
+
         def onward(t, carry):
-            s = zz + 1 + t // NC
+            s = zz + 2 + t // NC
             i = t % NC
             rows = pl.ds(chunk_base(i), C)
             rcopy(s, i, nxt).wait_recv()
@@ -271,7 +334,7 @@
         base = chunk_base(jnp.int32(i))
         rows = pl.ds(base, C)
 
-        @pl.when(hasp)
+        @pl.when(zz > 1)
         def _():
             rcopy(zz, i, nxt).wait_recv()
             att[rows, :] += res_in[zz, rows, :].astype(F32)
@@ -329,19 +392,33 @@
     for d in sendsA:
         d.wait_send()
 
-    @pl.when(hasp)
+    @pl.when(hasn)
+    def _():
+        for i in range(NC):
+            kcopy(i).wait_send()
+            vcopy(i).wait_send()
+
+    @pl.when(zz > 1)
+    def _():
+        for i in range(NC):
+            qcopy(zz, i, prv).wait_send()
+
+    @pl.when(hasp & hasn)
     def _():
         def fin(t, carry):
-            qcopy(zz + t // NC, t % NC, prv).wait_send()
+            qcopy(zz + 1 + t // NC, t % NC, prv).wait_send()
+            rcopy(zz + 1 + t // NC, t % NC, nxt).wait_send()
             return carry
 
         lax.fori_loop(0, items + NC, fin, 0)
 
-    def fin2(t, carry):
-        rcopy(zz + 1 + t // NC, t % NC, nxt).wait_send()
-        return carry
-
-    lax.fori_loop(0, items, fin2, 0)
+    @pl.when(zz == 0)
+    def _():
+        def fin(t, carry):
+            rcopy(2 + t // NC, t % NC, nxt).wait_send()
+            return carry
+
+        lax.fori_loop(0, items, fin, 0)
 
 
 def shards(events, norm_gain, w_uvqk, w_out, lengths):
@@ -360,12 +437,15 @@
         in_specs=[vspec] * 4 + [pl.BlockSpec(memory_space=pltpu.SMEM)],
         out_specs=vspec,
         scratch_shapes=[
-            vm((S, D), BF16), vm((T // 2, D), BF16), vm((S, HDIM), BF16), vm((S, HDIM), BF16), vm((S, HDIM), BF16),
+            vm((S, D), BF16), vm((T // 2, D), BF16), vm((HDIM, S), BF16), vm((T // 2, S), BF16), vm((S, HDIM), BF16),
+            vm((HDIM, S), BF16), vm((S, HDIM), BF16),
+            vm((S, HDIM), BF16),
             vm((line, S, HDIM), BF16), vm((line, S, HDIM), F32), vm((line, S, HDIM), BF16),
             vm((line, S, HDIM), BF16), vm((S, HDIM), F32), vm((S, HDIM), BF16), vm((T, D), BF16),
             vm((8, S), F32), vm((7, 8, T), F32), vm((D, F), BF16),
             dma((7, 2)), dma((7, 2)), dma((line, 4)), dma((line, 4)), dma((line, 4)), dma((line, 4)),
             dma((7, 2)), dma((7, 2)), dma((3,)), dma((3,)), dma((7,)), dma((7,)),
+            dma((4,)), dma((4,)), dma((4,)), dma((4,)),
         ],
         compiler_params=pltpu.CompilerParams(
             collective_id=0, has_side_effects=True, vmem_limit_bytes=56 * 1024 * 1024

time: 84.2 us -> 88.6 us (1.052)
  Pallas kernels: 79.1 us -> 83.5 us
    pallas_call x1, Pallas kernels: 79.1 us -> 83.5 us  [shards(): pl.pallas_call(functools.partial(kernel, line), out_shape=jax.ShapeDtypeS...]
where the time goes in v3:
time: 88.6 us; the launch traced here: 88.4 us
  Pallas kernels  83.5 us (94%)
  local copies, waits for them, and re-layouts  4.89 us (6%)
    pallas_call x1, Pallas kernels, shards(): pl.pallas_call(functools.partial(kernel, line), out_shape=jax.ShapeDtypeS...  83.5 us
    unnamed x4, local copies, waits for them, and re-layouts  4.53 us

profile of v3, /device:TPU:21, one launch (start us, length us, event | category | flops | bytes accessed | tf_op | source)
XLA Modules:
  0.0 88.4 jit_solution(14825803683707395033)
XLA Ops:
  0.0 0.0 copy-start
  0.0 1.6 %copy-done = bf16[1024,4,256]{2,1,0:T(4,128)(2,1)S(1)} copy-done((bf16[1024,4,256]{2,1,0:T(4,128)(2,1)S(1)}, bf16[1024,4,256]{2,1,0:T(4,128)(2,1)}, u32[]{:S(2)}) %copy-start) | copy-done | bytes 2097176
  1.6 0.4 constant_dynamic-slice_fusion
  2.0 1.2 %copy.8 = bf16[128,8,4,128]{3,1,2,0:T(8,128)(2,1)} copy(bf16[128,8,4,128]{3,2,1,0:T(4,128)(2,1)S(1)} %bitcast.5) | data formatting | bytes 2097152
  3.1 83.5 %shard_map.55 = bf16[768,256]{1,0:T(8,128)(2,1)} custom-call(bf16[768,256]{1,0:T(8,128)(2,1)} %ev.1, f32[1,1024]{1,0:T(1,128)} %bitcast.7, bf16[1024,512]{1,0:T(8,128)(2,1)} %bitcast.6, bf16[256,1024]{1,0:T(8,128)(2,1)} %wout.1, s32[8]{0:T(128)} %lengths.1), custom_call_target="tpu_custom_call" | custom-call | tf_op jit(solution)/shard_map/pallas_call | solution.py:434
  86.7 1.8 %copy.10 = bf16[768,256]{1,0:T(8,128)(2,1)} copy(bf16[768,256]{1,0:T(8,128)(2,1)} %shard_map.55) | data formatting | bytes 786432
Async XLA Ops:
  0.0 1.6 %copy-start = (bf16[1024,4,256]{2,1,0:T(4,128)(2,1)S(1)}, bf16[1024,4,256]{2,1,0:T(4,128)(2,1)}, u32[]{:S(2)}) copy-start(bf16[1024,4,256]{2,1,0:T(4,128)(2,1)} %param.7) | copy-start | bytes 6291460

commit v4 on v3

--- a/solution.py
+++ b/solution.py
@@ -247,6 +247,27 @@
     def _():
         lax.fori_loop(0, NC, passing, 0)
 
+    def pass_on(s, i):
+        rows = pl.ds(chunk_base(i), C)
+        return rc(res_in.at[s, rows], res_in.at[s, rows], rs.at[s, i], rr.at[s, i], nxt)
+
+    def straight(i, carry):
+        rcopy(zz + 1, i, nxt).wait_recv()
+        pass_on(zz + 1, i).start()
+        return carry
+
+    def onward(t, carry):
+        s = zz + 2 + t // NC
+        i = t % NC
+        rows = pl.ds(chunk_base(i), C)
+        rcopy(s, i, nxt).wait_recv()
+        res_out[s, rows, :] = (resf[s, rows, :] + res_in[s, rows, :].astype(F32)).astype(BF16)
+        rcopy(s, i, nxt).start()
+        return carry
+
+    items = jnp.where(zz < line - 2, NC * (line - 2 - zz), 0)
+    early = (zz == 1) & (items > 0)
+
     def incoming(t, carry):
         s = zz + 2 + t // NC
         i = t % NC
@@ -271,9 +292,12 @@
             res_out[s, rows, :] = total.astype(BF16)
             rcopy(s, i, nxt).start()
 
+        @pl.when(early & (t < NC))
+        def _():
+            straight(i, 0)
+
         return carry
 
-    items = jnp.where(zz < line - 2, NC * (line - 2 - zz), 0)
     lax.fori_loop(0, items, incoming, 0)
 
     @pl.when(hasp)
@@ -284,7 +308,15 @@
             kcopy(i).wait_recv()
             vcopy(i).wait_recv()
 
+        @pl.when(items > 0)
+        def _():
+            onward(0, 0)
+
         def crossing(i, carry):
+            @pl.when((items > 0) & (i < NC - 1))
+            def _():
+                onward(i + 1, 0)
+
             base = chunk_base(i)
             rows = pl.ds(base, C)
             _, start = starts_of(zz * SLAB + base)
@@ -293,29 +325,13 @@
 
         lax.fori_loop(0, NC, crossing, 0)
 
-    def pass_on(s, i):
-        rows = pl.ds(chunk_base(i), C)
-        return rc(res_in.at[s, rows], res_in.at[s, rows], rs.at[s, i], rr.at[s, i], nxt)
-
-    @pl.when(hasp & hasn)
-    def _():
-        def straight(i, carry):
-            rcopy(zz + 1, i, nxt).wait_recv()
-            pass_on(zz + 1, i).start()
-            return carry
-
+    @pl.when(hasp & hasn & jnp.logical_not(early))
+    def _():
         lax.fori_loop(0, NC, straight, 0)
 
-        def onward(t, carry):
-            s = zz + 2 + t // NC
-            i = t % NC
-            rows = pl.ds(chunk_base(i), C)
-            rcopy(s, i, nxt).wait_recv()
-            res_out[s, rows, :] = (resf[s, rows, :] + res_in[s, rows, :].astype(F32)).astype(BF16)
-            rcopy(s, i, nxt).start()
-            return carry
-
-        lax.fori_loop(0, items, onward, 0)
+    @pl.when(hasp)
+    def _():
+        lax.fori_loop(NC, jnp.maximum(items, NC), onward, 0)
 
     def epiece(xs, r, hs):
         return go.at[pl.ds(r * C, C), pl.ds(al(hs * F + xs * HDIM, HDIM), HDIM)]

time: 88.6 us -> 79.2 us (0.89)
  Pallas kernels: 83.5 us -> 74.1 us
    pallas_call x1, Pallas kernels: 83.5 us -> 74.1 us  [shards(): pl.pallas_call(functools.partial(kernel, line), out_shape=jax.ShapeDtypeS...]
where the time goes in v4:
time: 79.2 us; the launch traced here: 79 us
  Pallas kernels  74.1 us (94%)
  local copies, waits for them, and re-layouts  4.89 us (6%)
    pallas_call x1, Pallas kernels, shards(): pl.pallas_call(functools.partial(kernel, line), out_shape=jax.ShapeDtypeS...  74.1 us
    unnamed x4, local copies, waits for them, and re-layouts  4.53 us

profile of v4, /device:TPU:21, one launch (start us, length us, event | category | flops | bytes accessed | tf_op | source)
XLA Modules:
  0.0 79.0 jit_solution(10264719118699340815)
XLA Ops:
  0.0 0.0 copy-start
  0.0 1.6 %copy-done = bf16[1024,4,256]{2,1,0:T(4,128)(2,1)S(1)} copy-done((bf16[1024,4,256]{2,1,0:T(4,128)(2,1)S(1)}, bf16[1024,4,256]{2,1,0:T(4,128)(2,1)}, u32[]{:S(2)}) %copy-start) | copy-done | bytes 2097176
  1.6 0.4 constant_dynamic-slice_fusion
  2.0 1.2 %copy.8 = bf16[128,8,4,128]{3,1,2,0:T(8,128)(2,1)} copy(bf16[128,8,4,128]{3,2,1,0:T(4,128)(2,1)S(1)} %bitcast.5) | data formatting | bytes 2097152
  3.1 74.1 %shard_map.55 = bf16[768,256]{1,0:T(8,128)(2,1)} custom-call(bf16[768,256]{1,0:T(8,128)(2,1)} %ev.1, f32[1,1024]{1,0:T(1,128)} %bitcast.7, bf16[1024,512]{1,0:T(8,128)(2,1)} %bitcast.6, bf16[256,1024]{1,0:T(8,128)(2,1)} %wout.1, s32[8]{0:T(128)} %lengths.1), custom_call_target="tpu_custom_call" | custom-call | tf_op jit(solution)/shard_map/pallas_call | solution.py:450
  77.2 1.8 %copy.10 = bf16[768,256]{1,0:T(8,128)(2,1)} copy(bf16[768,256]{1,0:T(8,128)(2,1)} %shard_map.55) | data formatting | bytes 786432
Async XLA Ops:
  0.0 1.6 %copy-start = (bf16[1024,4,256]{2,1,0:T(4,128)(2,1)S(1)}, bf16[1024,4,256]{2,1,0:T(4,128)(2,1)}, u32[]{:S(2)}) copy-start(bf16[1024,4,256]{2,1,0:T(4,128)(2,1)} %param.7) | copy-start | bytes 6291460

commit v5 on v4

--- a/solution.py
+++ b/solution.py
@@ -116,6 +116,8 @@
         rows = pl.ds(chunk_base(i), C)
         return rc(vbuf.at[rows], vprev.at[rows], vs.at[i], vr.at[i], nxt)
 
+    half_scale = 0.5 * HDIM ** (-0.5)
+
     def project(i):
         base = chunk_base(i)
 
@@ -133,10 +135,10 @@
         for half in (1, 0):
             p = silu(
                 jnp.dot(nbuf[...], w[:, half * 2 * HDIM:(half + 1) * 2 * HDIM], preferred_element_type=F32)
-            ).astype(BF16)
+            )
             if half == 1:
-                qbuf[zz, rows, :] = p[:, :HDIM]
-                kbuf[:, rows] = p[:, HDIM:].astype(F32).T.astype(BF16)
+                qbuf[zz, rows, :] = (p[:, :HDIM] * half_scale).astype(BF16)
+                kbuf[:, rows] = p[:, HDIM:].T.astype(BF16)
 
                 @pl.when(zz > 1)
                 def _():
@@ -146,8 +148,8 @@
                 def _():
                     kcopy(i).start()
             else:
-                gate[rows, :] = p[:, :HDIM]
-                vbuf[rows, :] = p[:, HDIM:]
+                gate[rows, :] = p[:, :HDIM].astype(BF16)
+                vbuf[rows, :] = p[:, HDIM:].astype(BF16)
 
                 @pl.when(hasn)
                 def _():
@@ -185,8 +187,6 @@
         got(ox, r, h3, 3)
         project(2 + r)
 
-    half_scale = 0.5 * HDIM ** (-0.5)
-
     def starts_of(first):
         pos = first + lax.broadcasted_iota(jnp.int32, (C, 1), 0)
         end = jnp.int32(0)
@@ -197,7 +197,7 @@
         return pos, start
 
     def tile_weights(q, start, pos, k0, keys, first):
-        t = jnp.dot(q, keys[:, pl.ds(k0, KT)], preferred_element_type=F32) * half_scale
+        t = jnp.dot(q, keys[:, pl.ds(k0, KT)], preferred_element_type=F32)
         wgt = t + t * jnp.tanh(t)
         kpos = first + k0 + lax.broadcasted_iota(jnp.int32, (1, KT), 1)
         allowed = kpos >= start

time: 79.2 us -> 78.6 us (level)
  no operation moved by 1% of the time
where the time goes in v5:
time: 78.6 us; the launch traced here: 78.4 us
  Pallas kernels  73.5 us (94%)
  local copies, waits for them, and re-layouts  4.89 us (6%)
    pallas_call x1, Pallas kernels, shards(): pl.pallas_call(functools.partial(kernel, line), out_shape=jax.ShapeDtypeS...  73.5 us
    unnamed x4, local copies, waits for them, and re-layouts  4.53 us

profile of v5, /device:TPU:21, one launch (start us, length us, event | category | flops | bytes accessed | tf_op | source)
XLA Modules:
  0.0 78.4 jit_solution(13398756456721269108)
XLA Ops:
  0.0 0.0 copy-start
  0.0 1.6 %copy-done = bf16[1024,4,256]{2,1,0:T(4,128)(2,1)S(1)} copy-done((bf16[1024,4,256]{2,1,0:T(4,128)(2,1)S(1)}, bf16[1024,4,256]{2,1,0:T(4,128)(2,1)}, u32[]{:S(2)}) %copy-start) | copy-done | bytes 2097176
  1.6 0.4 constant_dynamic-slice_fusion
  2.0 1.2 %copy.8 = bf16[128,8,4,128]{3,1,2,0:T(8,128)(2,1)} copy(bf16[128,8,4,128]{3,2,1,0:T(4,128)(2,1)S(1)} %bitcast.5) | data formatting | bytes 2097152
  3.1 73.5 %shard_map.55 = bf16[768,256]{1,0:T(8,128)(2,1)} custom-call(bf16[768,256]{1,0:T(8,128)(2,1)} %ev.1, f32[1,1024]{1,0:T(1,128)} %bitcast.7, bf16[1024,512]{1,0:T(8,128)(2,1)} %bitcast.6, bf16[256,1024]{1,0:T(8,128)(2,1)} %wout.1, s32[8]{0:T(128)} %lengths.1), custom_call_target="tpu_custom_call" | custom-call | tf_op jit(solution)/shard_map/pallas_call | solution.py:450
  76.6 1.8 %copy.10 = bf16[768,256]{1,0:T(8,128)(2,1)} copy(bf16[768,256]{1,0:T(8,128)(2,1)} %shard_map.55) | data formatting | bytes 786432
Async XLA Ops:
  0.0 1.6 %copy-start = (bf16[1024,4,256]{2,1,0:T(4,128)(2,1)S(1)}, bf16[1024,4,256]{2,1,0:T(4,128)(2,1)}, u32[]{:S(2)}) copy-start(bf16[1024,4,256]{2,1,0:T(4,128)(2,1)} %param.7) | copy-start | bytes 6291460
